TPU v7x, 256 devices: a whole 4x4x8 slice. The times are simulated.
256 devices in a mesh: seq: 64 (over z, y, x_hi), fsdp: 4 (over x_lo, core).
Axes of the slice: x: 4 (x_hi: 2, x_lo: 2; x = x_hi * 2 + x_lo), y: 4, z: 8, core: 2. Of those that a mesh axis runs over, the one named last changes fastest.
Arguments:
- queries: bfloat16 [16384, 4096], P('seq', 'fsdp'), may hold values from -6 to 6
- keys: bfloat16 [16384, 4096], P('seq', 'fsdp'), may hold values from -6 to 6
- values: bfloat16 [16384, 4096], P('seq', 'fsdp'), may hold values from -6 to 6
- filters: float32 [16384, 4096], P('seq', 'fsdp'), as said below
- skip_weight: float32 [4096], P('fsdp'), may hold values from -4 to 4
- out_weight: bfloat16 [4096, 4096], P('fsdp'), may hold values from -0.125 to 0.125
Outputs:
- mixed_out: bfloat16 [16384, 4096], P('seq', 'fsdp')
Inputs may be any that keep to these rules, and one draw needn't show every extreme that they name: `filters`: real filter values of the 4096 channels at 16384 lags.
All inputs are finite; a program needn't handle non-finite values.
Results may differ from a plain program's by a relative error of at most 0.0049.
Values may be sent and summed in bfloat16 or wider, within the bound.
A program may use at most 128 MiB of HBM per device.

v0:
```python
import math

import jax
import jax.numpy as jnp
from jax import lax
from jax.sharding import PartitionSpec as P


def make_tables(n_peers, tok_rows):
    span = 2 * n_peers
    total = span * tok_rows
    outer = jnp.arange(span, dtype=jnp.int32)
    inner = jnp.arange(n_peers, dtype=jnp.int32)
    lagged = jnp.arange(tok_rows, dtype=jnp.int32)
    two_pi = 2.0 * math.pi
    angle_outer = two_pi * (outer[:, None] * inner[None, :] % span).astype(jnp.float32) / span
    angle_twist = two_pi * (outer[:, None] * lagged[None, :] % total).astype(jnp.float32) / total
    angle_inner = (
        two_pi * (lagged[:, None] * lagged[None, :] % tok_rows).astype(jnp.float32) / tok_rows
    )
    return (
        (jnp.cos(angle_outer), -jnp.sin(angle_outer)),
        (jnp.cos(angle_twist), -jnp.sin(angle_twist)),
        (jnp.cos(angle_inner), -jnp.sin(angle_inner)),
        total,
    )


def mat_last(field, table):
    return jnp.einsum("ckt,tm->ckm", field, table, precision=lax.Precision.HIGHEST)


def mat_outer(table, field):
    return jnp.einsum("ka,cat->ckt", table, field, precision=lax.Precision.HIGHEST)


def forward(signal, tables):
    (outer_re, outer_im), (twist_re, twist_im), (inner_re, inner_im), total = tables
    leading_real_part = mat_outer(outer_re, signal)
    first_im = mat_outer(outer_im, signal)
    turned_re = leading_real_part * twist_re - first_im * twist_im
    turned_im = leading_real_part * twist_im + first_im * twist_re
    spec_re = mat_last(turned_re, inner_re) - mat_last(turned_im, inner_im)
    spec_im = mat_last(turned_re, inner_im) + mat_last(turned_im, inner_re)
    return (spec_re, spec_im)


def inverse(spec_re, spec_im, tables):
    (outer_re, outer_im), (twist_re, twist_im), (inner_re, inner_im), total = tables
    back_re = mat_last(spec_re, inner_re) + mat_last(spec_im, inner_im)
    back_im = mat_last(spec_im, inner_re) - mat_last(spec_re, inner_im)
    turned_re = back_re * twist_re + back_im * twist_im
    turned_im = back_im * twist_re - back_re * twist_im
    result = jnp.einsum("ka,ckt->cat", outer_re, turned_re, precision=lax.Precision.HIGHEST)
    result = result + jnp.einsum(
        "ka,ckt->cat", outer_im, turned_im, precision=lax.Precision.HIGHEST
    )
    return result / total


def body(queries, keys, values, filters, skip_weight, out_weight):
    tok_rows = keys.shape[0]
    n_peers = lax.axis_size("seq")
    product = keys.astype(jnp.float32) * values.astype(jnp.float32)
    signal, kernel = (
        lax.all_to_all(product.T, "seq", split_axis=0, concat_axis=1, tiled=True),
        lax.all_to_all(filters.T, "seq", split_axis=0, concat_axis=1, tiled=True),
    )
    n_chans = signal.shape[0]
    signal = signal.reshape(n_chans, n_peers, tok_rows)
    kernel = kernel.reshape(n_chans, n_peers, tok_rows)
    tables = make_tables(n_peers, tok_rows)
    sig_re, sig_im = forward(signal, tables)
    ker_re, ker_im = forward(kernel, tables)
    prod_re = sig_re * ker_re - sig_im * ker_im
    prod_im = sig_re * ker_im + sig_im * ker_re
    conv = inverse(prod_re, prod_im, tables).reshape(n_chans, n_peers * tok_rows)
    returned = lax.all_to_all(conv, "seq", split_axis=1, concat_axis=0, tiled=True)
    mixed = returned.T + skip_weight[None, :] * product
    gated = (queries.astype(jnp.float32) * mixed).astype(jnp.bfloat16)
    columns = lax.all_to_all(out_weight, "fsdp", split_axis=1, concat_axis=0, tiled=True)
    whole = lax.all_gather(gated, "fsdp", axis=1, tiled=True)
    return jnp.dot(whole, columns, preferred_element_type=jnp.float32).astype(jnp.bfloat16)


def solution(mesh):
    in_specs = (
        P("seq", "fsdp"),
        P("seq", "fsdp"),
        P("seq", "fsdp"),
        P("seq", "fsdp"),
        P("fsdp"),
        P("fsdp", None),
    )
    out_specs = P("seq", "fsdp")
    return jax.shard_map(body, mesh=mesh, in_specs=in_specs, out_specs=out_specs, check_vma=False)
```

profile of v0, /device:TPU:1, one launch (start us, length us, event | category | flops | bytes accessed | tf_op | source)
XLA Modules:
  0.0 318.3 jit_solution(15699066041099765386)
XLA Ops:
  6.5 1.2 copy.60
  7.8 1.4 copy.61
  9.2 0.0 copy-start.6
  9.2 0.0 copy-start.9
  9.3 1.1 convert_multiply_fusion
  10.4 0.0 copy-done.6
  10.4 15.1 %all-to-all-start = ((f32[64,16,256]{2,1,0:T(8,128)}), f32[64,16,256]{2,1,0:T(8,128)S(1)}, u32[]{:S(2)}, u32[]{:S(2)}) async-start(f32[64,16,256]{2,1,0:T(8,128)} %bitcast.1), calls=%async_computation | async-start | bytes 2097152 | tf_op jit(solution)/shard_map/all_to_all | solution.py:66
  25.5 0.0 copy-done.9
  25.5 1.3 copy.65
  26.8 26.1 %all-to-all-done = f32[64,16,256]{2,1,0:T(8,128)S(1)} async-done(((f32[64,16,256]{2,1,0:T(8,128)}), f32[64,16,256]{2,1,0:T(8,128)S(1)}, u32[]{:S(2)}, u32[]{:S(2)}) %all-to-all-start) | async-done | bytes 1048608 | tf_op jit(solution)/shard_map/all_to_all | solution.py:66
  52.9 8.6 %all-to-all-start.1 = ((f32[64,16,256]{2,1,0:T(8,128)}), f32[64,16,256]{2,1,0:T(8,128)}, u32[]{:S(2)}, u32[]{:S(2)}) async-start(f32[64,16,256]{2,1,0:T(8,128)} %bitcast.10), calls=%async_computation.1 | async-start | bytes 2097152 | tf_op jit(solution)/shard_map/all_to_all | solution.py:67
  61.6 0.5 sine_negate_fusion.7
  62.1 0.1 copy.68
  62.2 0.8 copy.67
  63.0 3.8 %fusion.39 = f32[16,256,128]{2,1,0:T(8,128)S(1)} fusion(f32[64,16,256]{2,1,0:T(8,128)S(1)} %all-to-all-done), kind=kOutput, calls=%fused_computation.43 | convolution fusion | flops 402776064 | bytes 3145728 | tf_op jit(solution)/shard_map/ka,cat->ckt/dot_general | solution.py:34
  66.8 3.9 %fusion.41 = f32[16,256,128]{2,1,0:T(8,128)S(1)} fusion(f32[64,16,256]{2,1,0:T(8,128)S(1)} %all-to-all-done), kind=kOutput, calls=%fused_computation.45 | convolution fusion | flops 402767872 | bytes 3145728 | tf_op jit(solution)/shard_map/ka,cat->ckt/dot_general | solution.py:34
  70.7 6.4 %fusion.53 = f32[16,128,256]{2,1,0:T(8,128)} fusion(f32[16,256,128]{2,1,0:T(8,128)S(1)} %fusion.39, f32[16,256,128]{2,1,0:T(8,128)S(1)} %fusion.41, f32[128,256]{0,1:T(8,128)S(1)} %get-tuple-element.7, f32[128,256]{0,1:T(8,128)S(1)} %get-tuple-element.8), kind=kOutput, calls=%fused_computation.56 | convolution fusion | flops 1613168640 | bytes 6553600 | tf_op jit(solution)/shard_map/ckt,tm->ckm/dot_general | solution.py:30
  77.1 5.8 %fusion.55 = f32[16,128,256]{2,1,0:T(8,128)} fusion(f32[16,256,128]{2,1,0:T(8,128)S(1)} %fusion.39, f32[16,256,128]{2,1,0:T(8,128)S(1)} %fusion.41, f32[128,256]{0,1:T(8,128)S(1)} %get-tuple-element.7, f32[128,256]{0,1:T(8,128)S(1)} %get-tuple-element.8), kind=kOutput, calls=%fused_computation.57 | convolution fusion | flops 1613103104 | bytes 6553600 | tf_op jit(solution)/shard_map/ckt,tm->ckm/dot_general | solution.py:30
  82.9 5.3 %all-to-all-done.1 = f32[64,16,256]{2,1,0:T(8,128)} async-done(((f32[64,16,256]{2,1,0:T(8,128)}), f32[64,16,256]{2,1,0:T(8,128)}, u32[]{:S(2)}, u32[]{:S(2)}) %all-to-all-start.1) | async-done | bytes 1048608 | tf_op jit(solution)/shard_map/all_to_all | solution.py:67
  88.2 3.6 %fusion.35 = f32[128,16,256]{2,0,1:T(8,128)S(1)} fusion(f32[64,16,256]{2,1,0:T(8,128)} %all-to-all-done.1), kind=kOutput, calls=%fused_computation.39 | convolution fusion | flops 402776064 | bytes 3145728 | tf_op jit(solution)/shard_map/ka,cat->ckt/dot_general | solution.py:34
  91.9 3.7 %fusion.37 = f32[128,16,256]{2,0,1:T(8,128)S(1)} fusion(f32[64,16,256]{2,1,0:T(8,128)} %all-to-all-done.1), kind=kOutput, calls=%fused_computation.41 | convolution fusion | flops 402767872 | bytes 3145728 | tf_op jit(solution)/shard_map/ka,cat->ckt/dot_general | solution.py:34
  95.5 0.0 copy-done.8
  95.6 3.2 fusion
  98.8 3.0 fusion.2
  101.8 4.7 %convolution_subtract_fusion.1 = f32[16,128,256]{2,1,0:T(8,128)S(1)} fusion(f32[16,128,256]{2,1,0:T(8,128)S(1)} %copy-done.2, f32[16,256,128]{2,1,0:T(8,128)S(1)} %fusion.39, f32[16,256,128]{2,1,0:T(8,128)S(1)} %copy-done.1, f32[128,256]{0,1:T(8,128)S(1)} %get-tuple-element.7, f32[128,256]{0,1:T(8,128)S(1)} %get-tuple-element.8), kind=kOutput, calls=%fused_computation.31 | convolution fusion | flops 1613692928 | bytes 8650752 | tf_op jit(solution)/shard_map/ckt,tm->ckm/dot_general | solution.py:30
  106.5 3.1 fusion.21
  109.6 0.0 copy-start.3
  109.6 3.3 %fusion.18 = f32[16,128,256]{2,1,0:T(8,128)S(1)} fusion(f32[16,128,256]{2,1,0:T(8,128)S(1)} %fusion.2, f32[128,16,256]{2,0,1:T(8,128)S(1)} %fusion.35, f32[128,16,256]{2,0,1:T(8,128)S(1)} %fusion.37, f32[128,256]{1,0:T(8,128)S(1)} %copy.68, f32[128,256]{1,0:T(8,128)S(1)} %copy-done.8), kind=kOutput, calls=%fused_computation.26 | convolution fusion | flops 1613627392 | bytes 8650752 | tf_op jit(solution)/shard_map/ckt,tm->ckm/dot_general | solution.py:30
  113.0 0.0 copy-done.3
  113.0 5.1 %multiply_add_fusion = (f32[16,128,256]{2,1,0:T(8,128)S(1)}, f32[16,128,256]{2,1,0:T(8,128)S(1)}) fusion(f32[16,128,256]{2,1,0:T(8,128)S(1)} %fusion.18, f32[16,128,256]{2,1,0:T(8,128)S(1)} %convolution_subtract_fusion.1, f32[16,128,256]{2,1,0:T(8,128)S(1)} %fusion.21, f32[16,128,256]{2,1,0:T(8,128)S(1)} %copy-done.3, f32[16,256,128]{2,1,0:T(8,128)S(1)} %fusion.39, ...), kind=kOutput, calls=%fused_computation.22 | convolution fusion | flops 1616773120 | bytes 17039360 | tf_op jit(solution)/shard_map/ckt,tm->ckm/dot_general | solution.py:30
  118.1 3.0 fusion.66
  121.2 3.4 %fusion.68 = f32[16,128,256]{1,2,0:T(8,128)S(1)} fusion(f32[16,128,256]{2,1,0:T(8,128)S(1)} %get-tuple-element.6), kind=kOutput, calls=%fused_computation.72 | convolution fusion | flops 1611530240 | bytes 4194304 | tf_op jit(solution)/shard_map/ckt,tm->ckm/dot_general | solution.py:30
  124.6 3.0 convolution_subtract_fusion
  127.6 3.0 convolution_add_fusion
  130.7 2.8 fusion.10
  133.5 2.8 fusion.30
  136.3 1.8 copy.77
  138.0 8.2 %all-to-all-start.2 = ((f32[16,64,256]{2,0,1:T(8,128)}), f32[16,64,256]{2,0,1:T(8,128)S(1)}, u32[]{:S(2)}, u32[]{:S(2)}) async-start(f32[16,64,256]{2,0,1:T(8,128)} %copy.77), calls=%async_computation.2 | async-start | bytes 2097152 | tf_op jit(solution)/shard_map/all_to_all | solution.py:78
  146.3 11.5 %copy.78 = bf16[1024,4096]{0,1:T(8,128)(2,1)} copy(bf16[1024,4096]{1,0:T(8,128)(2,1)} %param.11) | data formatting | bytes 16777216 | tf_op args[5]
  157.8 15.3 %all-to-all-done.2 = f32[16,64,256]{2,0,1:T(8,128)S(1)} async-done(((f32[16,64,256]{2,0,1:T(8,128)}), f32[16,64,256]{2,0,1:T(8,128)S(1)}, u32[]{:S(2)}, u32[]{:S(2)}) %all-to-all-start.2) | async-done | bytes 1048608 | tf_op jit(solution)/shard_map/all_to_all | solution.py:78
  173.0 10.4 %all-to-all-start.3 = ((bf16[1024,4,1024]{0,2,1:T(8,128)(2,1)}), bf16[1024,4,1024]{0,2,1:T(8,128)(2,1)}, u32[]{:S(2)}, u32[]{:S(2)}) async-start(bf16[1024,4,1024]{0,2,1:T(8,128)(2,1)} %bitcast.120), calls=%async_computation.3 | async-start | bytes 16777216 | tf_op jit(solution)/shard_map/all_to_all | solution.py:81
  183.5 0.0 all-gather.2.cloned.1.call-start
  183.5 0.2 copy.59
  183.7 1.1 fusion.34
  184.8 0.0 all-gather.2.cloned.1.call-update
  184.8 107.9 %all-to-all-done.3 = bf16[1024,4,1024]{0,2,1:T(8,128)(2,1)} async-done(((bf16[1024,4,1024]{0,2,1:T(8,128)(2,1)}), bf16[1024,4,1024]{0,2,1:T(8,128)(2,1)}, u32[]{:S(2)}, u32[]{:S(2)}) %all-to-all-start.3) | async-done | bytes 8388640 | tf_op jit(solution)/shard_map/all_to_all | solution.py:81
  292.7 11.4 %copy.79 = bf16[4,1024,1024]{2,1,0:T(8,128)(2,1)} copy(bf16[4,1024,1024]{1,2,0:T(8,128)(2,1)} %bitcast.19) | data formatting | bytes 16777216 | tf_op jit(solution)/shard_map/all_to_all | solution.py:81
  304.0 7.2 %convolution_convert_fusion = bf16[256,1024]{1,0:T(8,128)(2,1)} fusion(bf16[256,4096]{0,1:T(8,128)(2,1)} %all-gather.2.cloned.1.call-done, bf16[4096,1024]{1,0:T(8,128)(2,1)} %bitcast.119), kind=kOutput, calls=%fused_computation.35 | convolution fusion | flops 2147745792 | bytes 11010048 | tf_op jit(solution)/shard_map/dot_general | solution.py:83
  (18 shorter events, 0.0 us)
Async XLA Ops:
  7.8 2.6 copy-start.4
  9.2 1.1 copy-start.6
  9.2 16.3 %copy-start.9 = (f32[256,1024]{1,0:T(8,128)S(1)}, f32[256,1024]{1,0:T(8,128)}, u32[]{:S(2)}) copy-start(f32[256,1024]{1,0:T(8,128)} %param.9) | copy-start | bytes 3145732
  10.4 42.6 %all-to-all-start = ((f32[64,16,256]{2,1,0:T(8,128)}), f32[64,16,256]{2,1,0:T(8,128)S(1)}, u32[]{:S(2)}, u32[]{:S(2)}) async-start(f32[64,16,256]{2,1,0:T(8,128)} %bitcast.1), calls=%async_computation | async-start | bytes 2097152 | tf_op jit(solution)/shard_map/all_to_all | solution.py:66
  52.9 35.3 %all-to-all-start.1 = ((f32[64,16,256]{2,1,0:T(8,128)}), f32[64,16,256]{2,1,0:T(8,128)}, u32[]{:S(2)}, u32[]{:S(2)}) async-start(f32[64,16,256]{2,1,0:T(8,128)} %bitcast.10), calls=%async_computation.1 | async-start | bytes 2097152 | tf_op jit(solution)/shard_map/all_to_all | solution.py:67
  70.7 6.4 %copy-start = (f32[16,256,128]{2,1,0:T(8,128)}, f32[16,256,128]{2,1,0:T(8,128)S(1)}, u32[]{:S(2)}) copy-start(f32[16,256,128]{2,1,0:T(8,128)S(1)} %fusion.41) | copy-start | bytes 6291460
  91.9 3.7 %copy-start.8 = (f32[128,256]{1,0:T(8,128)S(1)}, f32[128,256]{1,0:T(8,128)}, u32[]{:S(2)}) copy-start(f32[128,256]{1,0:T(8,128)} %copy.67) | copy-start | bytes 393220
  98.7 3.0 copy-start.1
  98.8 3.0 copy-start.2
  109.6 3.4 %copy-start.3 = (f32[16,128,256]{2,1,0:T(8,128)S(1)}, f32[16,128,256]{2,1,0:T(8,128)}, u32[]{:S(2)}) copy-start(f32[16,128,256]{2,1,0:T(8,128)} %fusion.53) | copy-start | bytes 6291460
  138.0 35.0 %all-to-all-start.2 = ((f32[16,64,256]{2,0,1:T(8,128)}), f32[16,64,256]{2,0,1:T(8,128)S(1)}, u32[]{:S(2)}, u32[]{:S(2)}) async-start(f32[16,64,256]{2,0,1:T(8,128)} %copy.77), calls=%async_computation.2 | async-start | bytes 2097152 | tf_op jit(solution)/shard_map/all_to_all | solution.py:78
  173.0 10.4 %copy-start.10 = (bf16[256,1024]{1,0:T(8,128)(2,1)S(1)}, bf16[256,1024]{1,0:T(8,128)(2,1)}, u32[]{:S(2)}) copy-start(bf16[256,1024]{1,0:T(8,128)(2,1)} %param.6) | copy-start | bytes 1572868
  173.0 10.7 %copy-start.5 = (bf16[256,1024]{0,1:T(8,128)(2,1)S(1)}, bf16[256,1024]{0,1:T(8,128)(2,1)}, u32[]{:S(2)}) copy-start(bf16[256,1024]{0,1:T(8,128)(2,1)} %copy-done.4) | copy-start | bytes 1572868
  173.0 10.7 %copy-start.7 = (bf16[256,1024]{0,1:T(8,128)(2,1)S(1)}, bf16[256,1024]{0,1:T(8,128)(2,1)}, u32[]{:S(2)}) copy-start(bf16[256,1024]{0,1:T(8,128)(2,1)} %copy-done.6) | copy-start | bytes 1572868
  173.0 10.7 %copy-start.11 = (f32[1024]{0:T(1024)S(1)}, f32[1024]{0:T(1024)}, u32[]{:S(2)}) copy-start(f32[1024]{0:T(1024)} %param.10) | copy-start | bytes 12292
  173.0 119.6 %all-to-all-start.3 = ((bf16[1024,4,1024]{0,2,1:T(8,128)(2,1)}), bf16[1024,4,1024]{0,2,1:T(8,128)(2,1)}, u32[]{:S(2)}, u32[]{:S(2)}) async-start(bf16[1024,4,1024]{0,2,1:T(8,128)(2,1)} %bitcast.120), calls=%async_computation.3 | async-start | bytes 16777216 | tf_op jit(solution)/shard_map/all_to_all | solution.py:81
  183.5 120.6 %all-gather.2.cloned.1.call-start = ((), (), s32[]{:S(2)}) async-start(), calls=%async_computation.4 | async-start | bytes 2621440 | tf_op jit(solution)/shard_map/all_gather | solution.py:82
Sparse Core Ops, SparseCore 0:
  186.1 44.3 all-gather.1
where the time goes:
time: 322 us; the launch traced here: 318 us
  waiting for transfers between devices  155 us (48%)
  matrix products  74.9 us (23%)
  starting transfers between devices  42.4 us (13%)
  local copies, waits for them, and re-layouts  29.8 us (9%)
  between operations  13.9 us (4%)
    all_to_all x1, waiting for transfers between devices, body(): lax.all_to_all(out_weight, 'fsdp', split_axis=1, concat_axis=0, tiled=True)  108 us
    dot_general x12, matrix products, mat_last(): jnp.einsum('ckt,tm->ckm', field, table, precision=lax.Precision.HIGHEST)  47.1 us
    all_to_all x1, waiting for transfers between devices, body(): lax.all_to_all(product.T, 'seq', split_axis=0, concat_axis=1, tiled=True)  26.1 us
    unnamed x29, local copies, waits for them, and re-layouts  15.8 us
    all_to_all x1, waiting for transfers between devices, body(): lax.all_to_all(conv, 'seq', split_axis=1, concat_axis=0, tiled=True)  15.3 us
    all_to_all x1, starting transfers between devices, body(): lax.all_to_all(product.T, 'seq', split_axis=0, concat_axis=1, tiled=True)  15.1 us
    dot_general x4, matrix products, mat_outer(): jnp.einsum('ka,cat->ckt', table, field, precision=lax.Precision.HIGHEST)  15 us
    all_to_all x1, local copies, waits for them, and re-layouts, body(): lax.all_to_all(out_weight, 'fsdp', split_axis=1, concat_axis=0, tiled=True)  11.4 us
  transfers between devices with their start and end apart: 5, of which 4 were waited for; matrix products, arithmetic and copies ran while one was open for 15% of the time, Pallas kernels for 0%

commit v1 on v0

v1 whole, which is shorter than its diff:
```python
import functools
import math

import jax
import jax.numpy as jnp
import ml_dtypes
import numpy as np
from jax import lax
from jax.experimental import pallas as pl
from jax.experimental.pallas import tpu as pltpu
from jax.sharding import PartitionSpec as P

MESH = pl.DeviceIdType.MESH
BF = jnp.bfloat16
F32 = jnp.float32
GROUP = 4


def split_np(table):
    high = table.astype(np.float32).astype(ml_dtypes.bfloat16)
    low = (table - high.astype(np.float64)).astype(np.float32).astype(ml_dtypes.bfloat16)
    return high, low


def make_tables(n_blocks, width):
    half = width // 2
    total = n_blocks * width
    theta = np.arange(n_blocks) + 0.25
    blocks = np.arange(n_blocks)
    lanes = np.arange(width)
    outer = 2 * math.pi * np.outer(theta, blocks) / n_blocks
    twist = 2 * math.pi * np.outer(theta, lanes) / total
    inner = 2 * math.pi * (np.outer(lanes, lanes) % width) / width
    cos, sin = np.cos(inner), np.sin(inner)
    fwd = np.block([[cos, -sin], [sin, cos]])
    inv = np.block([[cos, sin], [-sin, cos]])
    order = np.concatenate(
        [part * width + h * half + np.arange(half) for h in range(2) for part in range(2)]
    )
    inv = inv[:, order]
    first = np.concatenate([np.cos(outer), -np.sin(outer)], axis=0)
    last = np.concatenate([np.cos(outer).T, -np.sin(outer).T], axis=1) / total
    first_hi, first_lo = split_np(first)
    last_hi, last_lo = split_np(last)
    fwd_hi, fwd_lo = split_np(fwd)
    inv_hi, inv_lo = split_np(inv)
    return (
        np.concatenate([first_hi, first_lo], axis=1),
        np.cos(twist).astype(np.float32),
        (-np.sin(twist)).astype(np.float32),
        fwd_hi,
        fwd_lo,
        inv_hi,
        inv_lo,
        np.concatenate([last_hi, last_lo, last_hi], axis=1),
    )


def split(x):
    high = x.astype(BF)
    return high, (x - high.astype(F32)).astype(BF)


def mm(a, b):
    return jnp.dot(a, b, preferred_element_type=F32)


def kernel(*refs):
    hbm = refs[:14]
    out_ref = refs[14]
    vm = refs[15:29]
    (send_f, send_p, recv_f, recv_p, ret_s, ret_r, stage, z_hi, z_lo, p_hi, p_lo, spec,
     gated, mine, sib_s, sib_r, cross_s, cross_r,
     local_sem, fwd_send, fwd_recv, ret_send, ret_recv, pair_send, pair_recv) = refs[29:]
    filt, keys, vals, first, wre, wim, fwd_hi, fwd_lo, inv_hi, inv_lo, last, quer, skip, weight = vm

    me = lax.axis_index("seq")
    col = lax.axis_index("fsdp")
    n = send_f.shape[0]
    chans = send_f.shape[2]
    tok = keys.shape[0]
    half = tok // 2
    width = keys.shape[1]
    cols = out_ref.shape[1]
    block = min(128, width)
    peers = block // chans
    sibling = col + 1 - 2 * (col % 2)
    across = (col + 2) % 4
    beyond = (sibling + 2) % 4

    loads = [pltpu.make_async_copy(hbm[i], vm[i], local_sem.at[i]) for i in range(14)]
    for copy in loads:
        copy.start()

    barrier = pltpu.get_barrier_semaphore()

    def greet(i, carry):
        pl.semaphore_signal(
            barrier, inc=1, device_id={"seq": (me + i) % n}, device_id_type=MESH
        )
        return carry

    for other in (sibling, across):
        pl.semaphore_signal(barrier, inc=1, device_id={"fsdp": other}, device_id_type=MESH)
    lax.fori_loop(1, n, greet, 0)

    def spread(src, dst, send_sem, recv_sem):
        def go(i, carry):
            peer = (me + i) % n
            pltpu.make_async_remote_copy(
                src_ref=src.at[peer],
                dst_ref=dst.at[me],
                send_sem=send_sem,
                recv_sem=recv_sem,
                device_id={"seq": peer},
                device_id_type=MESH,
            ).start()
            return carry

        lax.fori_loop(1, n, go, 0)
        dst[me] = src[me]

    def landed(buf, sem):
        part = buf.at[pl.ds(0, n - 1)]
        pltpu.make_async_copy(part, part, sem).wait()

    loads[0].wait()
    for h in range(2):
        for j in range(width // block):
            x = filt[h * half:(h + 1) * half, j * block:(j + 1) * block]
            send_f[j * peers:(j + 1) * peers, h] = x.T.astype(BF).reshape(peers, chans, half)
    pl.semaphore_wait(barrier, n + 1)
    spread(send_f, recv_f, fwd_send.at[0], fwd_recv.at[0])
    loads[1].wait()
    loads[2].wait()
    for h in range(2):
        for j in range(width // block):
            rows, lanes = slice(h * half, (h + 1) * half), slice(j * block, (j + 1) * block)
            x = keys[rows, lanes].astype(F32) * vals[rows, lanes].astype(F32)
            send_p[j * peers:(j + 1) * peers, h] = x.T.astype(BF).reshape(peers, chans, half)
    spread(send_p, recv_p, fwd_send.at[1], fwd_recv.at[1])
    for i in range(3, 11):
        loads[i].wait()

    def forward(recv, sink):
        for h in range(2):
            stage[h] = recv[:, h].reshape(n * chans, half).astype(F32)
        for g in range(chans // GROUP):
            for cc in range(GROUP):
                c = g * GROUP + cc
                rows = slice(c * n, (c + 1) * n)
                for h in range(2):
                    lanes = slice(h * half, (h + 1) * half)
                    imag_lanes = slice(tok + h * half, tok + (h + 1) * half)
                    d = stage[h, pl.ds(c, n, stride=chans), :].astype(BF)
                    x = mm(first[...], jnp.concatenate([d, d], axis=0))
                    re, im = x[:n], x[n:]
                    wr, wi = wre[:, lanes], wim[:, lanes]
                    z_hi[rows, lanes], z_lo[rows, lanes] = split(re * wr - im * wi)
                    z_hi[rows, imag_lanes], z_lo[rows, imag_lanes] = split(re * wi + im * wr)
            rows = slice(g * GROUP * n, (g + 1) * GROUP * n)
            high, low = z_hi[rows], z_lo[rows]
            x = mm(high, fwd_hi[...]) + mm(low, fwd_hi[...]) + mm(high, fwd_lo[...])
            sink(rows, x)

    def keep(rows, x):
        spec[rows] = x

    def multiply(rows, x):
        xr, xi = x[:, :tok], x[:, tok:]
        hr, hi = spec[rows, :tok], spec[rows, tok:]
        p_hi[rows, :tok], p_lo[rows, :tok] = split(xr * hr - xi * hi)
        p_hi[rows, tok:], p_lo[rows, tok:] = split(xr * hi + xi * hr)

    landed(recv_f, fwd_recv.at[0])
    forward(recv_f, keep)
    landed(recv_p, fwd_recv.at[1])
    forward(recv_p, multiply)

    for h in range(2):
        lanes = slice(h * half, (h + 1) * half)
        sub = slice(h * tok, (h + 1) * tok)
        for g in range(chans // GROUP):
            rows = slice(g * GROUP * n, (g + 1) * GROUP * n)
            high, low = p_hi[rows], p_lo[rows]
            u = mm(high, inv_hi[:, sub]) + mm(low, inv_hi[:, sub]) + mm(high, inv_lo[:, sub])
            for cc in range(GROUP):
                c = g * GROUP + cc
                ur, ui = u[cc * n:(cc + 1) * n, :half], u[cc * n:(cc + 1) * n, half:]
                wr, wi = wre[:, lanes], wim[:, lanes]
                v = jnp.concatenate([ur * wr + ui * wi, ui * wr - ur * wi], axis=0)
                v_hi, v_lo = split(v)
                stage[h, pl.ds(c, n, stride=chans), :] = mm(
                    last[...], jnp.concatenate([v_hi, v_hi, v_lo], axis=0)
                )
        ret_s[h] = stage[h].astype(BF).reshape(n, chans, half)
        spread(ret_s.at[h], ret_r.at[h], ret_send.at[h], ret_recv.at[h])

    for i in range(11, 14):
        loads[i].wait()

    def partial(owner, tile):
        start = pl.multiple_of(owner * cols + tile * step, step)
        return mm(gated[...], weight[:, pl.ds(start, step)])

    step = min(256, cols)
    tiles = cols // step

    def pair(slot, h, src, dst, target):
        return pltpu.make_async_remote_copy(
            src_ref=src,
            dst_ref=dst,
            send_sem=pair_send.at[slot, h],
            recv_sem=pair_recv.at[slot, h],
            device_id={"fsdp": target},
            device_id_type=MESH,
        )

    def each_tile(body):
        @pl.loop(0, tiles)
        def _(t):
            body(t, pl.ds(pl.multiple_of(t * step, step), step))

    for h in range(2):
        rows = slice(h * half, (h + 1) * half)
        landed(ret_r.at[h], ret_recv.at[h])
        for j in range(width // block):
            lanes = slice(j * block, (j + 1) * block)
            conv = ret_r[h, j * peers:(j + 1) * peers].reshape(block, half).astype(F32).T
            product = keys[rows, lanes].astype(F32) * vals[rows, lanes].astype(F32)
            mixed = conv + skip[:, lanes] * product
            gated[:, lanes] = (quer[rows, lanes].astype(F32) * mixed).astype(BF)

        to_sib = pair(0, h, sib_s.at[0, h], sib_r.at[0, h], sibling)
        to_cross = pair(1, h, cross_s.at[h], cross_r.at[h], across)
        own_sib = pair(2, h, sib_s.at[1, h], sib_r.at[1, h], sibling)

        def far(t, at):
            sib_s[0, h, :, at] = partial(beyond, t).astype(BF)

        def near(t, at):
            mine[:, at] = partial(across, t)

        def sum_up(t, at):
            cross_s[h, :, at] = (mine[:, at] + sib_r[0, h, :, at].astype(F32)).astype(BF)

        def close(t, at):
            sib_s[1, h, :, at] = partial(sibling, t).astype(BF)

        def home(t, at):
            mine[:, at] = partial(col, t)

        def finish(t, at):
            out_ref[rows, at] = (
                mine[:, at] + sib_r[1, h, :, at].astype(F32) + cross_r[h, :, at].astype(F32)
            ).astype(BF)

        each_tile(far)
        to_sib.start()
        each_tile(near)
        to_sib.wait_recv()
        each_tile(sum_up)
        to_cross.start()
        each_tile(close)
        own_sib.start()
        each_tile(home)
        own_sib.wait_recv()
        to_cross.wait_recv()
        each_tile(finish)
        to_sib.wait_send()
        own_sib.wait_send()
        to_cross.wait_send()

    landed(send_f, fwd_send.at[0])
    landed(send_p, fwd_send.at[1])
    landed(ret_s.at[0], ret_send.at[0])
    landed(ret_s.at[1], ret_send.at[1])


def body(queries, keys, values, filters, skip_weight, out_weight):
    n = lax.axis_size("seq")
    tok, width = keys.shape
    cols = width
    half = tok // 2
    chans = width // n
    tables = make_tables(n, tok)
    first, wre, wim, fwd_hi, fwd_lo, inv_hi, inv_lo, last = [jnp.asarray(t) for t in tables]
    operands = (
        filters, keys, values, first, wre, wim, fwd_hi, fwd_lo, inv_hi, inv_lo, last,
        queries, skip_weight.reshape(1, width), out_weight,
    )
    dma = pltpu.SemaphoreType.DMA
    scratch = [pltpu.VMEM(x.shape, x.dtype) for x in operands] + [
        pltpu.VMEM((n, 2, chans, half), BF),
        pltpu.VMEM((n, 2, chans, half), BF),
        pltpu.VMEM((n, 2, chans, half), BF),
        pltpu.VMEM((n, 2, chans, half), BF),
        pltpu.VMEM((2, n, chans, half), BF),
        pltpu.VMEM((2, n, chans, half), BF),
        pltpu.VMEM((2, n * chans, half), F32),
        pltpu.VMEM((n * chans, 2 * tok), BF),
        pltpu.VMEM((n * chans, 2 * tok), BF),
        pltpu.VMEM((n * chans, 2 * tok), BF),
        pltpu.VMEM((n * chans, 2 * tok), BF),
        pltpu.VMEM((n * chans, 2 * tok), F32),
        pltpu.VMEM((half, width), BF),
        pltpu.VMEM((half, cols), F32),
        pltpu.VMEM((2, 2, half, cols), BF),
        pltpu.VMEM((2, 2, half, cols), BF),
        pltpu.VMEM((2, half, cols), BF),
        pltpu.VMEM((2, half, cols), BF),
        dma((14,)),
        dma((2,)),
        dma((2,)),
        dma((2,)),
        dma((2,)),
        dma((3, 2)),
        dma((3, 2)),
    ]
    flops = 2 * chans * n * 3 * (2 * tok) * (2 * tok) * 3 + 2 * tok * width * 4 * cols
    return pl.pallas_call(
        kernel,
        out_shape=jax.ShapeDtypeStruct((tok, cols), BF),
        in_specs=[pl.BlockSpec(memory_space=pl.ANY)] * len(operands),
        out_specs=pl.BlockSpec(memory_space=pltpu.VMEM),
        scratch_shapes=scratch,
        compiler_params=pltpu.CompilerParams(
            collective_id=0, has_side_effects=True, vmem_limit_bytes=48 * 1024 * 1024
        ),
        cost_estimate=pl.CostEstimate(
            flops=flops, bytes_accessed=16 * 1024 * 1024, transcendentals=0
        ),
        name="hyena",
    )(*operands)


def solution(mesh):
    in_specs = (
        P("seq", "fsdp"),
        P("seq", "fsdp"),
        P("seq", "fsdp"),
        P("seq", "fsdp"),
        P("fsdp"),
        P("fsdp", None),
    )
    out_specs = P("seq", "fsdp")
    return jax.shard_map(body, mesh=mesh, in_specs=in_specs, out_specs=out_specs, check_vma=False)
```

time: 322 us -> 93.7 us (0.29)
  waiting for transfers between devices: 155 us -> 0 us
  Pallas kernels: 0 us -> 79.7 us
  matrix products: 74.9 us -> 0 us
  starting transfers between devices: 42.4 us -> 0 us
  local copies, waits for them, and re-layouts: 29.8 us -> 13.2 us
  between operations: 13.9 us -> 0.02 us
    all_to_all x4 -> x0, waiting for transfers between devices: 155 us -> none  [the longest x1 108 us: body(): lax.all_to_all(out_weight, 'fsdp', split_axis=1, concat_axis=0, tiled=True)]
    pallas_call x0 -> x1, Pallas kernels: none -> 79.7 us  [body(): pl.pallas_call(kernel, out_shape=jax.ShapeDtypeStruct((tok, cols), BF), i...]
    dot_general x19 -> x0, matrix products: 74.9 us -> none  [the longest x12 47.1 us: mat_last(): jnp.einsum('ckt,tm->ckm', field, table, precision=lax.Precision.HIGHEST)]
    all_to_all x4 -> x0, starting transfers between devices: 42.4 us -> none  [the longest x1 15.1 us: body(): lax.all_to_all(product.T, 'seq', split_axis=0, concat_axis=1, tiled=True)]
    all_to_all x1 -> x0, local copies, waits for them, and re-layouts: 11.4 us -> none  [body(): lax.all_to_all(out_weight, 'fsdp', split_axis=1, concat_axis=0, tiled=True)]
    unnamed x29 -> x27, local copies, waits for them, and re-layouts: 15.8 us -> 13.2 us
  transfers between devices with their start and end apart: 5 -> 0, of which waited for: 4 -> 0; matrix products, arithmetic and copies ran while one was open for 15% -> 0% of each run, Pallas kernels for 0% -> 0%
where the time goes in v1:
time: 93.7 us; the launch traced here: 93 us
  Pallas kernels  79.7 us (85%)
  local copies, waits for them, and re-layouts  13.2 us (14%)
    pallas_call x1, Pallas kernels, body(): pl.pallas_call(kernel, out_shape=jax.ShapeDtypeStruct((tok, cols), BF), i...  79.7 us
    unnamed x27, local copies, waits for them, and re-layouts  13.2 us

profile of v1, /device:TPU:1, one launch (start us, length us, event | category | flops | bytes accessed | tf_op | source)
XLA Modules:
  0.0 93.0 jit_solution(10724296152797000290)
XLA Ops:
  0.0 0.0 copy-start
  0.0 1.2 %copy-done = f32[256,1024]{1,0:T(8,128)S(1)} copy-done((f32[256,1024]{1,0:T(8,128)S(1)}, f32[256,1024]{1,0:T(8,128)}, u32[]{:S(2)}) %copy-start) | copy-done | bytes 1048600
  1.2 0.0 copy-start.1
  1.2 1.0 %copy-done.1 = bf16[256,1024]{1,0:T(8,128)(2,1)S(1)} copy-done((bf16[256,1024]{1,0:T(8,128)(2,1)S(1)}, bf16[256,1024]{1,0:T(8,128)(2,1)}, u32[]{:S(2)}) %copy-start.1) | copy-done | bytes 524312
  2.3 0.0 copy-start.2
  2.3 1.0 %copy-done.2 = bf16[256,1024]{1,0:T(8,128)(2,1)S(1)} copy-done((bf16[256,1024]{1,0:T(8,128)(2,1)S(1)}, bf16[256,1024]{1,0:T(8,128)(2,1)}, u32[]{:S(2)}) %copy-start.2) | copy-done | bytes 524312
  3.3 0.0 copy-start.3
  3.3 1.0 %copy-done.3 = bf16[256,1024]{1,0:T(8,128)(2,1)S(1)} copy-done((bf16[256,1024]{1,0:T(8,128)(2,1)S(1)}, bf16[256,1024]{1,0:T(8,128)(2,1)}, u32[]{:S(2)}) %copy-start.3) | copy-done | bytes 524312
  4.4 0.0 copy-start.4
  4.4 0.7 copy-done.4
  5.0 0.0 copy-start.5
  5.0 1.0 %copy-done.5 = bf16[512,512]{1,0:T(8,128)(2,1)S(1)} copy-done((bf16[512,512]{1,0:T(8,128)(2,1)S(1)}, bf16[512,512]{1,0:T(8,128)(2,1)}, u32[]{:S(2)}) %copy-start.5) | copy-done | bytes 524312
  6.1 0.0 copy-start.6
  6.1 1.0 %copy-done.6 = bf16[512,512]{1,0:T(8,128)(2,1)S(1)} copy-done((bf16[512,512]{1,0:T(8,128)(2,1)S(1)}, bf16[512,512]{1,0:T(8,128)(2,1)}, u32[]{:S(2)}) %copy-start.6) | copy-done | bytes 524312
  7.1 0.0 copy-start.7
  7.1 1.0 %copy-done.7 = bf16[512,512]{1,0:T(8,128)(2,1)S(1)} copy-done((bf16[512,512]{1,0:T(8,128)(2,1)S(1)}, bf16[512,512]{1,0:T(8,128)(2,1)}, u32[]{:S(2)}) %copy-start.7) | copy-done | bytes 524312
  8.2 0.0 copy-start.8
  8.2 1.0 %copy-done.8 = bf16[512,512]{1,0:T(8,128)(2,1)S(1)} copy-done((bf16[512,512]{1,0:T(8,128)(2,1)S(1)}, bf16[512,512]{1,0:T(8,128)(2,1)}, u32[]{:S(2)}) %copy-start.8) | copy-done | bytes 524312
  9.2 0.0 copy-start.9
  9.2 0.8 copy-done.9
  10.0 0.0 copy-start.10
  10.1 0.8 copy-done.10
  10.9 0.0 copy-start.11
  10.9 0.8 copy-done.11
  11.7 0.0 copy-start.12
  11.7 0.8 copy-done.12
  12.4 79.7 %hyena.1 = bf16[256,1024]{1,0:T(8,128)(2,1)S(1)} custom-call(f32[256,1024]{1,0:T(8,128)S(1)} %copy-done, bf16[256,1024]{1,0:T(8,128)(2,1)S(1)} %copy-done.1, bf16[256,1024]{1,0:T(8,128)(2,1)S(1)} %copy-done.2, bf16[128,128]{1,0:T(8,128)(2,1)S(1)} %copy-done.12, f32[64,256]{1,0:T(8,128)S(1)} %copy-done.10, f32[64,256]{1,0:T(8,128)S(1)} %copy-done.9, ...), custom_call_target="tpu_custom_call" | custom-call | flops 6979321856 | bytes 16777216 | tf_op jit(solution)/shard_map/hyena/pallas_call | solution.py:321
  92.2 0.8 copy.16
Async XLA Ops:
  0.0 1.2 %copy-start = (f32[256,1024]{1,0:T(8,128)S(1)}, f32[256,1024]{1,0:T(8,128)}, u32[]{:S(2)}) copy-start(f32[256,1024]{1,0:T(8,128)} %refs_0_.1) | copy-start | bytes 3145732
  1.2 1.0 %copy-start.1 = (bf16[256,1024]{1,0:T(8,128)(2,1)S(1)}, bf16[256,1024]{1,0:T(8,128)(2,1)}, u32[]{:S(2)}) copy-start(bf16[256,1024]{1,0:T(8,128)(2,1)} %refs_1_.1) | copy-start | bytes 1572868
  2.3 1.0 %copy-start.2 = (bf16[256,1024]{1,0:T(8,128)(2,1)S(1)}, bf16[256,1024]{1,0:T(8,128)(2,1)}, u32[]{:S(2)}) copy-start(bf16[256,1024]{1,0:T(8,128)(2,1)} %refs_2_.1) | copy-start | bytes 1572868
  3.3 1.0 %copy-start.3 = (bf16[256,1024]{1,0:T(8,128)(2,1)S(1)}, bf16[256,1024]{1,0:T(8,128)(2,1)}, u32[]{:S(2)}) copy-start(bf16[256,1024]{1,0:T(8,128)(2,1)} %refs_11_.1) | copy-start | bytes 1572868
  4.4 0.7 copy-start.4
  5.0 1.0 %copy-start.5 = (bf16[512,512]{1,0:T(8,128)(2,1)S(1)}, bf16[512,512]{1,0:T(8,128)(2,1)}, u32[]{:S(2)}) copy-start(bf16[512,512]{1,0:T(8,128)(2,1)} %constant.22.clone.refs_9_) | copy-start | bytes 1572868
  6.1 1.0 %copy-start.6 = (bf16[512,512]{1,0:T(8,128)(2,1)S(1)}, bf16[512,512]{1,0:T(8,128)(2,1)}, u32[]{:S(2)}) copy-start(bf16[512,512]{1,0:T(8,128)(2,1)} %constant.21.clone.refs_8_) | copy-start | bytes 1572868
  7.1 1.0 %copy-start.7 = (bf16[512,512]{1,0:T(8,128)(2,1)S(1)}, bf16[512,512]{1,0:T(8,128)(2,1)}, u32[]{:S(2)}) copy-start(bf16[512,512]{1,0:T(8,128)(2,1)} %constant.20.clone.refs_7_) | copy-start | bytes 1572868
  8.2 1.0 %copy-start.8 = (bf16[512,512]{1,0:T(8,128)(2,1)S(1)}, bf16[512,512]{1,0:T(8,128)(2,1)}, u32[]{:S(2)}) copy-start(bf16[512,512]{1,0:T(8,128)(2,1)} %constant.19.clone.refs_6_) | copy-start | bytes 1572868
  9.2 0.8 copy-start.9
  10.0 0.8 copy-start.10
  10.9 0.8 copy-start.11
  11.7 0.8 copy-start.12

commit v2 on v1

--- a/solution.py
+++ b/solution.py
@@ -325,7 +325,7 @@
         out_specs=pl.BlockSpec(memory_space=pltpu.VMEM),
         scratch_shapes=scratch,
         compiler_params=pltpu.CompilerParams(
-            collective_id=0, has_side_effects=True, vmem_limit_bytes=48 * 1024 * 1024
+            collective_id=0, has_side_effects=True, vmem_limit_bytes=62 * 1024 * 1024
         ),
         cost_estimate=pl.CostEstimate(
             flops=flops, bytes_accessed=16 * 1024 * 1024, transcendentals=0

time: 93.7 us -> 81.9 us (0.87)
  local copies, waits for them, and re-layouts: 13.2 us -> 1.87 us
    unnamed x27 -> x1, local copies, waits for them, and re-layouts: 13.2 us -> 1.87 us
where the time goes in v2:
time: 81.9 us; the launch traced here: 81.8 us
  Pallas kernels  79.9 us (98%)
  local copies, waits for them, and re-layouts  1.87 us (2%)
    pallas_call x1, Pallas kernels, body(): pl.pallas_call(kernel, out_shape=jax.ShapeDtypeStruct((tok, cols), BF), i...  79.9 us
    unnamed x1, local copies, waits for them, and re-layouts  1.87 us

profile of v2, /device:TPU:1, one launch (start us, length us, event | category | flops | bytes accessed | tf_op | source)
XLA Modules:
  0.0 81.8 jit_solution(15062339110482764404)
XLA Ops:
  0.0 79.9 %hyena.1 = bf16[256,1024]{1,0:T(8,128)(2,1)} custom-call(f32[256,1024]{1,0:T(8,128)} %refs_0_.1, bf16[256,1024]{1,0:T(8,128)(2,1)} %refs_1_.1, bf16[256,1024]{1,0:T(8,128)(2,1)} %refs_2_.1, bf16[128,128]{1,0:T(8,128)(2,1)} %constant.16.clone.refs_3_, f32[64,256]{1,0:T(8,128)} %constant.17.clone.refs_4_, f32[64,256]{1,0:T(8,128)} %constant.18.clone.refs_5_, ...), custom_call_target="tpu_custom_call" | custom-call | flops 6979321856 | bytes 16777216 | tf_op jit(solution)/shard_map/hyena/pallas_call | solution.py:321
  80.0 1.9 %copy.16 = bf16[256,1024]{1,0:T(8,128)(2,1)} copy(bf16[256,1024]{1,0:T(8,128)(2,1)} %hyena.1) | data formatting | bytes 1048576

commit v3 on v2

--- a/solution.py
+++ b/solution.py
@@ -14,6 +14,7 @@
 BF = jnp.bfloat16
 F32 = jnp.float32
 GROUP = 4
+PARTS = 2
 
 
 def split_np(table):
@@ -70,7 +71,7 @@
     out_ref = refs[14]
     vm = refs[15:29]
     (send_f, send_p, recv_f, recv_p, ret_s, ret_r, stage, z_hi, z_lo, p_hi, p_lo, spec,
-     gated, mine, sib_s, sib_r, cross_s, cross_r,
+     gated, mine, sib_s, sib_r, own_s, own_r, cross_s, cross_r,
      local_sem, fwd_send, fwd_recv, ret_send, ret_recv, pair_send, pair_recv) = refs[29:]
     filt, keys, vals, first, wre, wim, fwd_hi, fwd_lo, inv_hi, inv_lo, last, quer, skip, weight = vm
 
@@ -199,12 +200,7 @@
     for i in range(11, 14):
         loads[i].wait()
 
-    def partial(owner, tile):
-        start = pl.multiple_of(owner * cols + tile * step, step)
-        return mm(gated[...], weight[:, pl.ds(start, step)])
-
-    step = min(256, cols)
-    tiles = cols // step
+    part = cols // PARTS
 
     def pair(slot, h, src, dst, target):
         return pltpu.make_async_remote_copy(
@@ -216,61 +212,69 @@
             device_id_type=MESH,
         )
 
-    def each_tile(body):
-        @pl.loop(0, tiles)
-        def _(t):
-            body(t, pl.ds(pl.multiple_of(t * step, step), step))
-
-    for h in range(2):
+    def partial(h, owner, piece):
+        start = pl.multiple_of(owner * cols + piece * part, part)
+        return mm(gated[h], weight[:, pl.ds(start, part)])
+
+    def to_sib(h, piece):
+        return pair(piece, h, sib_s.at[h, piece], sib_r.at[h, piece], sibling)
+
+    def to_cross(h, piece):
+        return pair(PARTS + piece, h, cross_s.at[h, piece], cross_r.at[h, piece], across)
+
+    def own_sib(h, piece):
+        return pair(2 * PARTS + piece, h, own_s.at[h, piece], own_r.at[h, piece], sibling)
+
+    def gate(h):
         rows = slice(h * half, (h + 1) * half)
-        landed(ret_r.at[h], ret_recv.at[h])
         for j in range(width // block):
             lanes = slice(j * block, (j + 1) * block)
             conv = ret_r[h, j * peers:(j + 1) * peers].reshape(block, half).astype(F32).T
             product = keys[rows, lanes].astype(F32) * vals[rows, lanes].astype(F32)
             mixed = conv + skip[:, lanes] * product
-            gated[:, lanes] = (quer[rows, lanes].astype(F32) * mixed).astype(BF)
-
-        to_sib = pair(0, h, sib_s.at[0, h], sib_r.at[0, h], sibling)
-        to_cross = pair(1, h, cross_s.at[h], cross_r.at[h], across)
-        own_sib = pair(2, h, sib_s.at[1, h], sib_r.at[1, h], sibling)
-
-        def far(t, at):
-            sib_s[0, h, :, at] = partial(beyond, t).astype(BF)
-
-        def near(t, at):
-            mine[:, at] = partial(across, t)
-
-        def sum_up(t, at):
-            cross_s[h, :, at] = (mine[:, at] + sib_r[0, h, :, at].astype(F32)).astype(BF)
-
-        def close(t, at):
-            sib_s[1, h, :, at] = partial(sibling, t).astype(BF)
-
-        def home(t, at):
-            mine[:, at] = partial(col, t)
-
-        def finish(t, at):
-            out_ref[rows, at] = (
-                mine[:, at] + sib_r[1, h, :, at].astype(F32) + cross_r[h, :, at].astype(F32)
+            gated[h, :, lanes] = (quer[rows, lanes].astype(F32) * mixed).astype(BF)
+
+    def leave(h):
+        for piece in range(PARTS):
+            sib_s[h, piece] = partial(h, beyond, piece).astype(BF)
+            to_sib(h, piece).start()
+        for piece in range(PARTS):
+            near = partial(h, across, piece)
+            to_sib(h, piece).wait_recv()
+            cross_s[h, piece] = (near + sib_r[h, piece].astype(F32)).astype(BF)
+            to_cross(h, piece).start()
+
+    def stay(h):
+        for piece in range(PARTS):
+            own_s[h, piece] = partial(h, sibling, piece).astype(BF)
+            own_sib(h, piece).start()
+        for piece in range(PARTS):
+            mine[h, piece] = partial(h, col, piece)
+
+    def finish(h):
+        rows = slice(h * half, (h + 1) * half)
+        for piece in range(PARTS):
+            own_sib(h, piece).wait_recv()
+            to_cross(h, piece).wait_recv()
+            out_ref[rows, piece * part:(piece + 1) * part] = (
+                mine[h, piece] + own_r[h, piece].astype(F32) + cross_r[h, piece].astype(F32)
             ).astype(BF)
 
-        each_tile(far)
-        to_sib.start()
-        each_tile(near)
-        to_sib.wait_recv()
-        each_tile(sum_up)
-        to_cross.start()
-        each_tile(close)
-        own_sib.start()
-        each_tile(home)
-        own_sib.wait_recv()
-        to_cross.wait_recv()
-        each_tile(finish)
-        to_sib.wait_send()
-        own_sib.wait_send()
-        to_cross.wait_send()
-
+    landed(ret_r.at[0], ret_recv.at[0])
+    gate(0)
+    leave(0)
+    stay(0)
+    landed(ret_r.at[1], ret_recv.at[1])
+    gate(1)
+    leave(1)
+    stay(1)
+    finish(0)
+    finish(1)
+    for h in range(2):
+        for piece in range(PARTS):
+            to_sib(h, piece).wait_send()
+            to_cross(h, piece).wait_send()
+            own_sib(h, piece).wait_send()
     landed(send_f, fwd_send.at[0])
     landed(send_p, fwd_send.at[1])
     landed(ret_s.at[0], ret_send.at[0])
@@ -303,19 +307,21 @@
         pltpu.VMEM((n * chans, 2 * tok), BF),
         pltpu.VMEM((n * chans, 2 * tok), BF),
         pltpu.VMEM((n * chans, 2 * tok), F32),
-        pltpu.VMEM((half, width), BF),
-        pltpu.VMEM((half, cols), F32),
-        pltpu.VMEM((2, 2, half, cols), BF),
-        pltpu.VMEM((2, 2, half, cols), BF),
-        pltpu.VMEM((2, half, cols), BF),
-        pltpu.VMEM((2, half, cols), BF),
+        pltpu.VMEM((2, half, width), BF),
+        pltpu.VMEM((2, PARTS, half, cols // PARTS), F32),
+        pltpu.VMEM((2, PARTS, half, cols // PARTS), BF),
+        pltpu.VMEM((2, PARTS, half, cols // PARTS), BF),
+        pltpu.VMEM((2, PARTS, half, cols // PARTS), BF),
+        pltpu.VMEM((2, PARTS, half, cols // PARTS), BF),
+        pltpu.VMEM((2, PARTS, half, cols // PARTS), BF),
+        pltpu.VMEM((2, PARTS, half, cols // PARTS), BF),
         dma((14,)),
         dma((2,)),
         dma((2,)),
         dma((2,)),
         dma((2,)),
-        dma((3, 2)),
-        dma((3, 2)),
+        dma((3 * PARTS, 2)),
+        dma((3 * PARTS, 2)),
     ]
     flops = 2 * chans * n * 3 * (2 * tok) * (2 * tok) * 3 + 2 * tok * width * 4 * cols
     return pl.pallas_call(

time: 81.9 us -> 75.9 us (0.927)
  Pallas kernels: 79.9 us -> 73.9 us
    pallas_call x1, Pallas kernels: 79.9 us -> 73.9 us  [body(): pl.pallas_call(kernel, out_shape=jax.ShapeDtypeStruct((tok, cols), BF), i...]
where the time goes in v3:
time: 75.9 us; the launch traced here: 75.8 us
  Pallas kernels  73.9 us (97%)
  local copies, waits for them, and re-layouts  1.87 us (2%)
    pallas_call x1, Pallas kernels, body(): pl.pallas_call(kernel, out_shape=jax.ShapeDtypeStruct((tok, cols), BF), i...  73.9 us
    unnamed x1, local copies, waits for them, and re-layouts  1.87 us

profile of v3, /device:TPU:1, one launch (start us, length us, event | category | flops | bytes accessed | tf_op | source)
XLA Modules:
  0.0 75.8 jit_solution(6626290840815663727)
XLA Ops:
  0.0 73.9 %hyena.1 = bf16[256,1024]{1,0:T(8,128)(2,1)} custom-call(f32[256,1024]{1,0:T(8,128)} %refs_0_.1, bf16[256,1024]{1,0:T(8,128)(2,1)} %refs_1_.1, bf16[256,1024]{1,0:T(8,128)(2,1)} %refs_2_.1, bf16[128,128]{1,0:T(8,128)(2,1)} %constant.16.clone.refs_3_, f32[64,256]{1,0:T(8,128)} %constant.17.clone.refs_4_, f32[64,256]{1,0:T(8,128)} %constant.18.clone.refs_5_, ...), custom_call_target="tpu_custom_call" | custom-call | flops 6979321856 | bytes 16777216 | tf_op jit(solution)/shard_map/hyena/pallas_call | solution.py:327
  73.9 1.9 %copy.16 = bf16[256,1024]{1,0:T(8,128)(2,1)} copy(bf16[256,1024]{1,0:T(8,128)(2,1)} %hyena.1) | data formatting | bytes 1048576

commit v4 on v3

--- a/solution.py
+++ b/solution.py
@@ -15,6 +15,7 @@
 F32 = jnp.float32
 GROUP = 4
 PARTS = 2
+CHUNKS = 2
 
 
 def split_np(table):
@@ -27,32 +28,24 @@
     half = width // 2
     total = n_blocks * width
     theta = np.arange(n_blocks) + 0.25
-    blocks = np.arange(n_blocks)
-    lanes = np.arange(width)
-    outer = 2 * math.pi * np.outer(theta, blocks) / n_blocks
-    twist = 2 * math.pi * np.outer(theta, lanes) / total
-    inner = 2 * math.pi * (np.outer(lanes, lanes) % width) / width
+    lanes = np.arange(half)
+    outer = 2 * math.pi * np.outer(theta, np.arange(n_blocks)) / n_blocks
+    twist = 2 * math.pi * np.outer(theta, np.arange(width)) / total
+    inner = 2 * math.pi * (np.outer(lanes, lanes) % half) / half
     cos, sin = np.cos(inner), np.sin(inner)
-    fwd = np.block([[cos, -sin], [sin, cos]])
-    inv = np.block([[cos, sin], [-sin, cos]])
-    order = np.concatenate(
-        [part * width + h * half + np.arange(half) for h in range(2) for part in range(2)]
-    )
-    inv = inv[:, order]
+    turn = 2 * math.pi * lanes[None, :] / width
     first = np.concatenate([np.cos(outer), -np.sin(outer)], axis=0)
     last = np.concatenate([np.cos(outer).T, -np.sin(outer).T], axis=1) / total
     first_hi, first_lo = split_np(first)
     last_hi, last_lo = split_np(last)
-    fwd_hi, fwd_lo = split_np(fwd)
-    inv_hi, inv_lo = split_np(inv)
     return (
         np.concatenate([first_hi, first_lo], axis=1),
         np.cos(twist).astype(np.float32),
         (-np.sin(twist)).astype(np.float32),
-        fwd_hi,
-        fwd_lo,
-        inv_hi,
-        inv_lo,
+        np.cos(turn).astype(np.float32),
+        (-np.sin(turn)).astype(np.float32),
+        *split_np(np.block([[cos, -sin], [sin, cos]])),
+        *split_np(np.block([[cos, sin], [-sin, cos]])),
         np.concatenate([last_hi, last_lo, last_hi], axis=1),
     )
 
@@ -67,13 +60,14 @@
 
 
 def kernel(*refs):
-    hbm = refs[:14]
-    out_ref = refs[14]
-    vm = refs[15:29]
-    (send_f, send_p, recv_f, recv_p, ret_s, ret_r, stage, z_hi, z_lo, p_hi, p_lo, spec,
+    hbm = refs[:16]
+    out_ref = refs[16]
+    vm = refs[17:33]
+    (send_f, send_p, recv_f, recv_p, ret_s, ret_r, stage, conv_f, z_hi, z_lo, waves, spec,
      gated, mine, sib_s, sib_r, own_s, own_r, cross_s, cross_r,
-     local_sem, fwd_send, fwd_recv, ret_send, ret_recv, pair_send, pair_recv) = refs[29:]
-    filt, keys, vals, first, wre, wim, fwd_hi, fwd_lo, inv_hi, inv_lo, last, quer, skip, weight = vm
+     local_sem, fwd_send, fwd_recv, ret_send, ret_recv, pair_send, pair_recv) = refs[33:]
+    (filt, keys, vals, first, wre, wim, ure, uim, fwd_hi, fwd_lo, inv_hi, inv_lo, last,
+     quer, skip, weight) = vm
 
     me = lax.axis_index("seq")
     col = lax.axis_index("fsdp")
@@ -83,14 +77,15 @@
     half = tok // 2
     width = keys.shape[1]
     cols = out_ref.shape[1]
+    some = chans // CHUNKS
     block = min(128, width)
     peers = block // chans
     sibling = col + 1 - 2 * (col % 2)
     across = (col + 2) % 4
     beyond = (sibling + 2) % 4
 
-    loads = [pltpu.make_async_copy(hbm[i], vm[i], local_sem.at[i]) for i in range(14)]
-    for copy in loads:
+    loads = [pltpu.make_async_copy(hbm[i], vm[i], local_sem.at[i]) for i in range(16)]
+    for copy in loads[:3]:
         copy.start()
 
     barrier = pltpu.get_barrier_semaphore()
@@ -132,72 +127,116 @@
             send_f[j * peers:(j + 1) * peers, h] = x.T.astype(BF).reshape(peers, chans, half)
     pl.semaphore_wait(barrier, n + 1)
     spread(send_f, recv_f, fwd_send.at[0], fwd_recv.at[0])
+    for copy in loads[3:13]:
+        copy.start()
     loads[1].wait()
     loads[2].wait()
+    for j in range(width // block):
+        lanes = slice(j * block, (j + 1) * block)
+        turned = []
+        for h in range(2):
+            rows = slice(h * half, (h + 1) * half)
+            x = keys[rows, lanes].astype(F32) * vals[rows, lanes].astype(F32)
+            turned.append(x.T.reshape(peers, chans, half))
+        for q in range(CHUNKS):
+            sub = slice(q * some, (q + 1) * some)
+            send_p[q, j * peers:(j + 1) * peers] = jnp.concatenate(
+                [x[:, sub] for x in turned], axis=1
+            ).astype(BF)
+    for q in range(CHUNKS):
+        spread(send_p.at[q], recv_p.at[q], fwd_send.at[1 + q], fwd_recv.at[1 + q])
+    for copy in loads[13:]:
+        copy.start()
+    for i in range(3, 13):
+        loads[i].wait()
+
+    def rotate(x, y, wr, wi):
+        return x * wr - y * wi, x * wi + y * wr
+
+    def outer(c, read):
+        d = jnp.concatenate([read(h) for h in range(2)], axis=1).astype(BF)
+        x = mm(first[...], jnp.concatenate([d, d], axis=0))
+        ar, ai = rotate(x[:n, :half], x[n:, :half], wre[:, :half], wim[:, :half])
+        br, bi = rotate(x[:n, half:], x[n:, half:], wre[:, half:], wim[:, half:])
+        odd_r, odd_i = rotate(ar - br, ai - bi, ure[...], uim[...])
+        rows = slice(c * n, (c + 1) * n)
+        for i, value in enumerate((ar + br, ai + bi, odd_r, odd_i)):
+            lanes = slice(i * half, (i + 1) * half)
+            z_hi[rows, lanes], z_lo[rows, lanes] = split(value)
+
+    def inner(rows, lanes, high_table, low_table):
+        high, low = z_hi[rows, lanes], z_lo[rows, lanes]
+        return mm(high, high_table[...]) + mm(low, high_table[...]) + mm(high, low_table[...])
+
+    def group_rows(g):
+        return slice(g * GROUP * n, (g + 1) * GROUP * n)
+
+    both = [slice(par * tok, (par + 1) * tok) for par in range(2)]
+
+    def keep(g):
+        for lanes in both:
+            spec[group_rows(g), lanes] = inner(group_rows(g), lanes, fwd_hi, fwd_lo)
+
+    def multiply(g):
+        for lanes in both:
+            x, hx = inner(group_rows(g), lanes, fwd_hi, fwd_lo), spec[group_rows(g), lanes]
+            pr, pi = rotate(x[:, :half], x[:, half:], hx[:, :half], hx[:, half:])
+            z_hi[group_rows(g), lanes], z_lo[group_rows(g), lanes] = split(
+                jnp.concatenate([pr, pi], axis=1)
+            )
+
+    def back(g):
+        even = inner(group_rows(g), both[0], inv_hi, inv_lo)
+        odd = inner(group_rows(g), both[1], inv_hi, inv_lo)
+        tr, ti = rotate(odd[:, :half], odd[:, half:], ure[...], -uim[...])
+        odd = jnp.concatenate([tr, ti], axis=1)
+        waves[0, group_rows(g)] = even + odd
+        waves[1, group_rows(g)] = even - odd
+
+    def close_up(g, h):
+        lanes = slice(h * half, (h + 1) * half)
+        for c in range(g * GROUP, (g + 1) * GROUP, 2):
+            sides = []
+            for cc in (c, c + 1):
+                u = waves[h, cc * n:(cc + 1) * n]
+                vr, vi = rotate(u[:, :half], u[:, half:], wre[:, lanes], -wim[:, lanes])
+                sides.append(jnp.concatenate([vr, vi], axis=0))
+            v_hi, v_lo = split(jnp.concatenate(sides, axis=1))
+            y = mm(last[...], jnp.concatenate([v_hi, v_hi, v_lo], axis=0))
+            conv_f[h, pl.ds(c, n, stride=chans), :] = y[:, :half]
+            conv_f[h, pl.ds(c + 1, n, stride=chans), :] = y[:, half:]
+
+    groups = chans // GROUP
+    landed(recv_f, fwd_recv.at[0])
     for h in range(2):
-        for j in range(width // block):
-            rows, lanes = slice(h * half, (h + 1) * half), slice(j * block, (j + 1) * block)
-            x = keys[rows, lanes].astype(F32) * vals[rows, lanes].astype(F32)
-            send_p[j * peers:(j + 1) * peers, h] = x.T.astype(BF).reshape(peers, chans, half)
-    spread(send_p, recv_p, fwd_send.at[1], fwd_recv.at[1])
-    for i in range(3, 11):
-        loads[i].wait()
-
-    def forward(recv, sink):
+        stage[h] = recv_f[:, h].reshape(n * chans, half).astype(F32)
+    for g in range(groups):
+        for c in range(g * GROUP, (g + 1) * GROUP):
+            outer(c, lambda h: stage[h, pl.ds(c, n, stride=chans), :])
+    for g in range(groups):
+        keep(g)
+
+    for q in range(CHUNKS):
+        landed(recv_p.at[q], fwd_recv.at[1 + q])
+        stage[q] = recv_p[q].reshape(n * 2 * some, half).astype(F32)
+        mine_now = range(q * groups // CHUNKS, (q + 1) * groups // CHUNKS)
+        for g in mine_now:
+            for c in range(g * GROUP, (g + 1) * GROUP):
+                outer(c, lambda h: stage[
+                    q, pl.ds(h * some + c - q * some, n, stride=2 * some), :
+                ])
+        for g in mine_now:
+            multiply(g)
+        for g in mine_now:
+            back(g)
         for h in range(2):
-            stage[h] = recv[:, h].reshape(n * chans, half).astype(F32)
-        for g in range(chans // GROUP):
-            for cc in range(GROUP):
-                c = g * GROUP + cc
-                rows = slice(c * n, (c + 1) * n)
-                for h in range(2):
-                    lanes = slice(h * half, (h + 1) * half)
-                    imag_lanes = slice(tok + h * half, tok + (h + 1) * half)
-                    d = stage[h, pl.ds(c, n, stride=chans), :].astype(BF)
-                    x = mm(first[...], jnp.concatenate([d, d], axis=0))
-                    re, im = x[:n], x[n:]
-                    wr, wi = wre[:, lanes], wim[:, lanes]
-                    z_hi[rows, lanes], z_lo[rows, lanes] = split(re * wr - im * wi)
-                    z_hi[rows, imag_lanes], z_lo[rows, imag_lanes] = split(re * wi + im * wr)
-            rows = slice(g * GROUP * n, (g + 1) * GROUP * n)
-            high, low = z_hi[rows], z_lo[rows]
-            x = mm(high, fwd_hi[...]) + mm(low, fwd_hi[...]) + mm(high, fwd_lo[...])
-            sink(rows, x)
-
-    def keep(rows, x):
-        spec[rows] = x
-
-    def multiply(rows, x):
-        xr, xi = x[:, :tok], x[:, tok:]
-        hr, hi = spec[rows, :tok], spec[rows, tok:]
-        p_hi[rows, :tok], p_lo[rows, :tok] = split(xr * hr - xi * hi)
-        p_hi[rows, tok:], p_lo[rows, tok:] = split(xr * hi + xi * hr)
-
-    landed(recv_f, fwd_recv.at[0])
-    forward(recv_f, keep)
-    landed(recv_p, fwd_recv.at[1])
-    forward(recv_p, multiply)
-
-    for h in range(2):
-        lanes = slice(h * half, (h + 1) * half)
-        sub = slice(h * tok, (h + 1) * tok)
-        for g in range(chans // GROUP):
-            rows = slice(g * GROUP * n, (g + 1) * GROUP * n)
-            high, low = p_hi[rows], p_lo[rows]
-            u = mm(high, inv_hi[:, sub]) + mm(low, inv_hi[:, sub]) + mm(high, inv_lo[:, sub])
-            for cc in range(GROUP):
-                c = g * GROUP + cc
-                ur, ui = u[cc * n:(cc + 1) * n, :half], u[cc * n:(cc + 1) * n, half:]
-                wr, wi = wre[:, lanes], wim[:, lanes]
-                v = jnp.concatenate([ur * wr + ui * wi, ui * wr - ur * wi], axis=0)
-                v_hi, v_lo = split(v)
-                stage[h, pl.ds(c, n, stride=chans), :] = mm(
-                    last[...], jnp.concatenate([v_hi, v_hi, v_lo], axis=0)
-                )
-        ret_s[h] = stage[h].astype(BF).reshape(n, chans, half)
-        spread(ret_s.at[h], ret_r.at[h], ret_send.at[h], ret_recv.at[h])
-
-    for i in range(11, 14):
+            for g in mine_now:
+                close_up(g, h)
+            if q == CHUNKS - 1:
+                ret_s[h] = conv_f[h].astype(BF).reshape(n, chans, half)
+                spread(ret_s.at[h], ret_r.at[h], ret_send.at[h], ret_recv.at[h])
+
+    for i in range(13, 16):
         loads[i].wait()
 
     part = cols // PARTS
@@ -276,7 +315,8 @@
             to_cross(h, piece).wait_send()
             own_sib(h, piece).wait_send()
     landed(send_f, fwd_send.at[0])
-    landed(send_p, fwd_send.at[1])
+    for q in range(CHUNKS):
+        landed(send_p.at[q], fwd_send.at[1 + q])
     landed(ret_s.at[0], ret_send.at[0])
     landed(ret_s.at[1], ret_send.at[1])
 
@@ -287,25 +327,23 @@
     cols = width
     half = tok // 2
     chans = width // n
-    tables = make_tables(n, tok)
-    first, wre, wim, fwd_hi, fwd_lo, inv_hi, inv_lo, last = [jnp.asarray(t) for t in tables]
+    tables = [jnp.asarray(t) for t in make_tables(n, tok)]
     operands = (
-        filters, keys, values, first, wre, wim, fwd_hi, fwd_lo, inv_hi, inv_lo, last,
-        queries, skip_weight.reshape(1, width), out_weight,
+        filters, keys, values, *tables, queries, skip_weight.reshape(1, width), out_weight,
     )
     dma = pltpu.SemaphoreType.DMA
     scratch = [pltpu.VMEM(x.shape, x.dtype) for x in operands] + [
         pltpu.VMEM((n, 2, chans, half), BF),
+        pltpu.VMEM((CHUNKS, n, 2 * chans // CHUNKS, half), BF),
         pltpu.VMEM((n, 2, chans, half), BF),
-        pltpu.VMEM((n, 2, chans, half), BF),
-        pltpu.VMEM((n, 2, chans, half), BF),
+        pltpu.VMEM((CHUNKS, n, 2 * chans // CHUNKS, half), BF),
         pltpu.VMEM((2, n, chans, half), BF),
         pltpu.VMEM((2, n, chans, half), BF),
         pltpu.VMEM((2, n * chans, half), F32),
+        pltpu.VMEM((2, n * chans, half), F32),
         pltpu.VMEM((n * chans, 2 * tok), BF),
         pltpu.VMEM((n * chans, 2 * tok), BF),
-        pltpu.VMEM((n * chans, 2 * tok), BF),
-        pltpu.VMEM((n * chans, 2 * tok), BF),
+        pltpu.VMEM((2, n * chans, tok), F32),
         pltpu.VMEM((n * chans, 2 * tok), F32),
         pltpu.VMEM((2, half, width), BF),
         pltpu.VMEM((2, PARTS, half, cols // PARTS), F32),
@@ -315,15 +353,15 @@
         pltpu.VMEM((2, PARTS, half, cols // PARTS), BF),
         pltpu.VMEM((2, PARTS, half, cols // PARTS), BF),
         pltpu.VMEM((2, PARTS, half, cols // PARTS), BF),
-        dma((14,)),
-        dma((2,)),
-        dma((2,)),
+        dma((16,)),
+        dma((1 + CHUNKS,)),
+        dma((1 + CHUNKS,)),
         dma((2,)),
         dma((2,)),
         dma((3 * PARTS, 2)),
         dma((3 * PARTS, 2)),
     ]
-    flops = 2 * chans * n * 3 * (2 * tok) * (2 * tok) * 3 + 2 * tok * width * 4 * cols
+    flops = 2 * chans * n * 3 * (2 * tok) * tok * 3 + 2 * tok * width * 4 * cols
     return pl.pallas_call(
         kernel,
         out_shape=jax.ShapeDtypeStruct((tok, cols), BF),

time: 75.9 us -> 71.1 us (0.937)
  Pallas kernels: 73.9 us -> 69 us
    pallas_call x1, Pallas kernels: 73.9 us -> 69 us  [body(): pl.pallas_call(kernel, out_shape=jax.ShapeDtypeStruct((tok, cols), BF), i...]
where the time goes in v4:
time: 71.1 us; the launch traced here: 70.9 us
  Pallas kernels  69 us (97%)
  local copies, waits for them, and re-layouts  1.87 us (3%)
    pallas_call x1, Pallas kernels, body(): pl.pallas_call(kernel, out_shape=jax.ShapeDtypeStruct((tok, cols), BF), i...  69 us
    unnamed x1, local copies, waits for them, and re-layouts  1.87 us

profile of v4, /device:TPU:1, one launch (start us, length us, event | category | flops | bytes accessed | tf_op | source)
XLA Modules:
  0.0 70.9 jit_solution(8683109502984291888)
XLA Ops:
  0.0 69.0 %hyena.1 = bf16[256,1024]{1,0:T(8,128)(2,1)} custom-call(f32[256,1024]{1,0:T(8,128)} %refs_0_.1, bf16[256,1024]{1,0:T(8,128)(2,1)} %refs_1_.1, bf16[256,1024]{1,0:T(8,128)(2,1)} %refs_2_.1, bf16[128,128]{1,0:T(8,128)(2,1)} %constant.20.clone.refs_3_, f32[64,256]{1,0:T(8,128)} %constant.21.clone.refs_4_, f32[64,256]{1,0:T(8,128)} %constant.22.clone.refs_5_, ...), custom_call_target="tpu_custom_call" | custom-call | flops 4563402752 | bytes 16777216 | tf_op jit(solution)/shard_map/hyena/pallas_call | solution.py:365
  69.0 1.9 %copy.18 = bf16[256,1024]{1,0:T(8,128)(2,1)} copy(bf16[256,1024]{1,0:T(8,128)(2,1)} %hyena.1) | data formatting | bytes 1048576

commit v5 on v4

--- a/solution.py
+++ b/solution.py
@@ -14,8 +14,10 @@
 BF = jnp.bfloat16
 F32 = jnp.float32
 GROUP = 4
-PARTS = 2
+PARTS = 4
+FIRST = 2
 CHUNKS = 2
+ORDER = (4, 3, 5, 2, 6, 1, 7, 0)
 
 
 def split_np(table):
@@ -113,7 +115,9 @@
             ).start()
             return carry
 
-        lax.fori_loop(1, n, go, 0)
+        run = min(8, n)
+        for at in ORDER if n == 64 else range(n // run):
+            lax.fori_loop(max(1, at * run), (at + 1) * run, go, 0)
         dst[me] = src[me]
 
     def landed(buf, sem):
@@ -241,79 +245,86 @@
 
     part = cols // PARTS
 
-    def pair(slot, h, src, dst, target):
+    def pair(slot, src, dst, target):
         return pltpu.make_async_remote_copy(
             src_ref=src,
             dst_ref=dst,
-            send_sem=pair_send.at[slot, h],
-            recv_sem=pair_recv.at[slot, h],
+            send_sem=pair_send.at[slot],
+            recv_sem=pair_recv.at[slot],
             device_id={"fsdp": target},
             device_id_type=MESH,
         )
 
-    def partial(h, owner, piece):
+    def partial(rows, owner, piece):
         start = pl.multiple_of(owner * cols + piece * part, part)
-        return mm(gated[h], weight[:, pl.ds(start, part)])
-
-    def to_sib(h, piece):
-        return pair(piece, h, sib_s.at[h, piece], sib_r.at[h, piece], sibling)
-
-    def to_cross(h, piece):
-        return pair(PARTS + piece, h, cross_s.at[h, piece], cross_r.at[h, piece], across)
-
-    def own_sib(h, piece):
-        return pair(2 * PARTS + piece, h, own_s.at[h, piece], own_r.at[h, piece], sibling)
+        return mm(gated[rows], weight[:, pl.ds(start, part)])
+
+    def token_rows(h):
+        return slice(h * half, (h + 1) * half)
+
+    def to_sib(h, p):
+        return pair(h * PARTS + p, sib_s.at[h, p], sib_r.at[h, p], sibling)
+
+    def to_cross(h, p):
+        return pair((2 + h) * PARTS + p, cross_s.at[h, p], cross_r.at[h, p], across)
+
+    def own_sib(p):
+        return pair(4 * PARTS + p, own_s.at[p], own_r.at[p], sibling)
 
     def gate(h):
-        rows = slice(h * half, (h + 1) * half)
+        rows = token_rows(h)
         for j in range(width // block):
             lanes = slice(j * block, (j + 1) * block)
             conv = ret_r[h, j * peers:(j + 1) * peers].reshape(block, half).astype(F32).T
             product = keys[rows, lanes].astype(F32) * vals[rows, lanes].astype(F32)
             mixed = conv + skip[:, lanes] * product
-            gated[h, :, lanes] = (quer[rows, lanes].astype(F32) * mixed).astype(BF)
-
-    def leave(h):
-        for piece in range(PARTS):
-            sib_s[h, piece] = partial(h, beyond, piece).astype(BF)
-            to_sib(h, piece).start()
-        for piece in range(PARTS):
-            near = partial(h, across, piece)
-            to_sib(h, piece).wait_recv()
-            cross_s[h, piece] = (near + sib_r[h, piece].astype(F32)).astype(BF)
-            to_cross(h, piece).start()
-
-    def stay(h):
-        for piece in range(PARTS):
-            own_s[h, piece] = partial(h, sibling, piece).astype(BF)
-            own_sib(h, piece).start()
-        for piece in range(PARTS):
-            mine[h, piece] = partial(h, col, piece)
-
-    def finish(h):
-        rows = slice(h * half, (h + 1) * half)
-        for piece in range(PARTS):
-            own_sib(h, piece).wait_recv()
-            to_cross(h, piece).wait_recv()
-            out_ref[rows, piece * part:(piece + 1) * part] = (
-                mine[h, piece] + own_r[h, piece].astype(F32) + cross_r[h, piece].astype(F32)
-            ).astype(BF)
+            gated[rows, lanes] = (quer[rows, lanes].astype(F32) * mixed).astype(BF)
+
+    def far(h, p):
+        sib_s[h, p] = partial(token_rows(h), beyond, p).astype(BF)
+        to_sib(h, p).start()
+
+    def near(h, p):
+        own = partial(token_rows(h), across, p)
+        to_sib(h, p).wait_recv()
+        cross_s[h, p] = (own + sib_r[h, p].astype(F32)).astype(BF)
+        to_cross(h, p).start()
 
     landed(ret_r.at[0], ret_recv.at[0])
     gate(0)
-    leave(0)
-    stay(0)
+    for p in range(PARTS):
+        far(0, p)
+    for p in range(FIRST):
+        near(0, p)
     landed(ret_r.at[1], ret_recv.at[1])
     gate(1)
-    leave(1)
-    stay(1)
-    finish(0)
-    finish(1)
+    for p in range(PARTS):
+        far(1, p)
+    for p in range(FIRST, PARTS):
+        near(0, p)
+    for p in range(PARTS):
+        near(1, p)
+    everything = slice(0, tok)
+    for p in range(PARTS):
+        own_s[p] = partial(everything, sibling, p).astype(BF)
+        own_sib(p).start()
+    for p in range(PARTS):
+        mine[p] = partial(everything, col, p)
+    for p in range(PARTS):
+        own_sib(p).wait_recv()
+        mine[p] += own_r[p].astype(F32)
     for h in range(2):
-        for piece in range(PARTS):
-            to_sib(h, piece).wait_send()
-            to_cross(h, piece).wait_send()
-            own_sib(h, piece).wait_send()
+        for p in range(PARTS):
+            to_cross(h, p).wait_recv()
+            out_ref[token_rows(h), p * part:(p + 1) * part] = (
+                mine[p, token_rows(h)] + cross_r[h, p].astype(F32)
+            ).astype(BF)
+    for p in range(PARTS):
+        own_sib(p).wait_send()
+        for h in range(2):
+            to_sib(h, p).wait_send()
+            to_cross(h, p).wait_send()
+
     landed(send_f, fwd_send.at[0])
     for q in range(CHUNKS):
         landed(send_p.at[q], fwd_send.at[1 + q])
@@ -345,12 +356,12 @@
         pltpu.VMEM((n * chans, 2 * tok), BF),
         pltpu.VMEM((2, n * chans, tok), F32),
         pltpu.VMEM((n * chans, 2 * tok), F32),
-        pltpu.VMEM((2, half, width), BF),
-        pltpu.VMEM((2, PARTS, half, cols // PARTS), F32),
+        pltpu.VMEM((tok, width), BF),
+        pltpu.VMEM((PARTS, tok, cols // PARTS), F32),
         pltpu.VMEM((2, PARTS, half, cols // PARTS), BF),
         pltpu.VMEM((2, PARTS, half, cols // PARTS), BF),
-        pltpu.VMEM((2, PARTS, half, cols // PARTS), BF),
-        pltpu.VMEM((2, PARTS, half, cols // PARTS), BF),
+        pltpu.VMEM((PARTS, tok, cols // PARTS), BF),
+        pltpu.VMEM((PARTS, tok, cols // PARTS), BF),
         pltpu.VMEM((2, PARTS, half, cols // PARTS), BF),
         pltpu.VMEM((2, PARTS, half, cols // PARTS), BF),
         dma((16,)),
@@ -358,8 +369,8 @@
         dma((1 + CHUNKS,)),
         dma((2,)),
         dma((2,)),
-        dma((3 * PARTS, 2)),
-        dma((3 * PARTS, 2)),
+        dma((5 * PARTS,)),
+        dma((5 * PARTS,)),
     ]
     flops = 2 * chans * n * 3 * (2 * tok) * tok * 3 + 2 * tok * width * 4 * cols
     return pl.pallas_call(

time: 71.1 us -> 69.9 us (0.983)
  Pallas kernels: 69 us -> 67.9 us
    pallas_call x1, Pallas kernels: 69 us -> 67.9 us  [body(): pl.pallas_call(kernel, out_shape=jax.ShapeDtypeStruct((tok, cols), BF), i...]
where the time goes in v5:
time: 69.9 us; the launch traced here: 69.8 us
  Pallas kernels  67.9 us (97%)
  local copies, waits for them, and re-layouts  1.87 us (3%)
    pallas_call x1, Pallas kernels, body(): pl.pallas_call(kernel, out_shape=jax.ShapeDtypeStruct((tok, cols), BF), i...  67.9 us
    unnamed x1, local copies, waits for them, and re-layouts  1.87 us

profile of v5, /device:TPU:1, one launch (start us, length us, event | category | flops | bytes accessed | tf_op | source)
XLA Modules:
  0.0 69.8 jit_solution(12831322963816784250)
XLA Ops:
  0.0 67.9 %hyena.1 = bf16[256,1024]{1,0:T(8,128)(2,1)} custom-call(f32[256,1024]{1,0:T(8,128)} %refs_0_.1, bf16[256,1024]{1,0:T(8,128)(2,1)} %refs_1_.1, bf16[256,1024]{1,0:T(8,128)(2,1)} %refs_2_.1, bf16[128,128]{1,0:T(8,128)(2,1)} %constant.20.clone.refs_3_, f32[64,256]{1,0:T(8,128)} %constant.21.clone.refs_4_, f32[64,256]{1,0:T(8,128)} %constant.22.clone.refs_5_, ...), custom_call_target="tpu_custom_call" | custom-call | flops 4563402752 | bytes 16777216 | tf_op jit(solution)/shard_map/hyena/pallas_call | solution.py:376
  67.9 1.9 %copy.18 = bf16[256,1024]{1,0:T(8,128)(2,1)} copy(bf16[256,1024]{1,0:T(8,128)(2,1)} %hyena.1) | data formatting | bytes 1048576

commit v6 on v5

--- a/solution.py
+++ b/solution.py
@@ -14,8 +14,8 @@
 BF = jnp.bfloat16
 F32 = jnp.float32
 GROUP = 4
-PARTS = 4
-FIRST = 2
+PARTS = 2
+FIRST = 1
 CHUNKS = 2
 ORDER = (4, 3, 5, 2, 6, 1, 7, 0)
 

time: 69.9 us -> 69.8 us (level)
  no operation moved by 1% of the time
where the time goes in v6:
time: 69.8 us; the launch traced here: 69.7 us
  Pallas kernels  67.8 us (97%)
  local copies, waits for them, and re-layouts  1.87 us (3%)
    pallas_call x1, Pallas kernels, body(): pl.pallas_call(kernel, out_shape=jax.ShapeDtypeStruct((tok, cols), BF), i...  67.8 us
    unnamed x1, local copies, waits for them, and re-layouts  1.87 us

profile of v6, /device:TPU:1, one launch (start us, length us, event | category | flops | bytes accessed | tf_op | source)
XLA Modules:
  0.0 69.7 jit_solution(16961059744514172087)
XLA Ops:
  0.0 67.8 %hyena.1 = bf16[256,1024]{1,0:T(8,128)(2,1)} custom-call(f32[256,1024]{1,0:T(8,128)} %refs_0_.1, bf16[256,1024]{1,0:T(8,128)(2,1)} %refs_1_.1, bf16[256,1024]{1,0:T(8,128)(2,1)} %refs_2_.1, bf16[128,128]{1,0:T(8,128)(2,1)} %constant.20.clone.refs_3_, f32[64,256]{1,0:T(8,128)} %constant.21.clone.refs_4_, f32[64,256]{1,0:T(8,128)} %constant.22.clone.refs_5_, ...), custom_call_target="tpu_custom_call" | custom-call | flops 4563402752 | bytes 16777216 | tf_op jit(solution)/shard_map/hyena/pallas_call | solution.py:376
  67.8 1.9 %copy.18 = bf16[256,1024]{1,0:T(8,128)(2,1)} copy(bf16[256,1024]{1,0:T(8,128)(2,1)} %hyena.1) | data formatting | bytes 1048576
